TPU v7x, 256 devices: a whole 4x4x8 slice. The times are simulated.
256 devices in a mesh: group: 16 (over y, x), member: 16 (over z, core).
Axes of the slice: x: 4, y: 4, z: 8, core: 2. Of those that a mesh axis runs over, the one named last changes fastest.
Arguments:
- tokens: bfloat16 [32768, 1024], P(('group', 'member')), may hold values from -420 to 420
- latents: bfloat16 [1024, 1024], P('member'), may hold values from -420 to 420
- tok_gain: float32 [1024], replicated, may hold values from 0.5 to 1.5
- lat_gain: float32 [1024], replicated, may hold values from 0.5 to 1.5
- mlp_gain: float32 [1024], replicated, may hold values from 0.5 to 1.5
- w_ref_tok: bfloat16 [1024, 1024], replicated, may hold values from -1.15625 to 1.15625
- w_val_tok: bfloat16 [1024, 1024], replicated, may hold values from -0.75 to 0.75
- w_out_tok: bfloat16 [1024, 1024], replicated, may hold values from -0.1875 to 0.1875
- w_ref_lat: bfloat16 [1024, 1024], P('member'), may hold values from -1.15625 to 1.15625
- w_val_lat: bfloat16 [1024, 1024], P('member'), may hold values from -0.75 to 0.75
- w_out_lat: bfloat16 [1024, 1024], P('member'), may hold values from -0.1875 to 0.1875
- w_up: bfloat16 [1024, 2048], P(None, 'member'), may hold values from -0.1875 to 0.1875
- w_down: bfloat16 [2048, 1024], P('member'), may hold values from -0.125 to 0.125
Outputs:
- tokens_out: bfloat16 [32768, 1024], P(('group', 'member'))
- latents_out: bfloat16 [1024, 1024], P('member')
All inputs are finite; a program needn't handle non-finite values.
Results may differ from a plain program's by a relative error of at most 0.005.
The roundings to bfloat16 on the way count: a program that leaves them out, or rounds other values in their place, can miss the bound.
Values may be sent and summed in bfloat16 or wider, within the bound.
A program may use at most 128 MiB of HBM per device.

v0:
```python
import jax
import jax.numpy as jnp
from jax import lax
from jax.sharding import PartitionSpec as P

HEAD_DIM = 64


NORM_EPS = 1e-06
BLOCK_HEADS = 4


def normalize(values):
    return values * lax.rsqrt(jnp.mean(values * values, axis=-1, keepdims=True) + NORM_EPS)


def project(left_side, right_side):
    return jnp.dot(left_side, right_side, preferred_element_type=jnp.float32)


def head_slice(matrix, first_col):
    piece = lax.slice_in_dim(matrix, first_col, first_col + BLOCK_HEADS * HEAD_DIM, axis=1)
    return piece.reshape(matrix.shape[0], BLOCK_HEADS, HEAD_DIM)


def head_scores(ref_tok, ref_lat, first_col):
    attention_scores = jnp.einsum(
        "ngd,mgd->gnm",
        head_slice(ref_tok, first_col),
        head_slice(ref_lat, first_col),
        preferred_element_type=jnp.float32,
    )
    return attention_scores * HEAD_DIM ** (-0.5)


def row_part(attention_scores, val_lat, first_col):
    highest = jnp.max(attention_scores, axis=2, keepdims=True)
    exponent = jnp.exp(attention_scores - highest)
    weights = (exponent / jnp.sum(exponent, axis=2, keepdims=True)).astype(jnp.bfloat16)
    mixed = jnp.einsum(
        "gnm,mgd->ngd", weights, head_slice(val_lat, first_col), preferred_element_type=jnp.float32
    )
    return mixed.reshape(mixed.shape[0], BLOCK_HEADS * HEAD_DIM)


def column_part(attention_scores, shift, val_tok, first_col):
    exponent = jnp.exp(attention_scores - shift[:, None, :])
    upper = lax.optimization_barrier(exponent.astype(jnp.bfloat16))
    lower = (exponent - upper.astype(jnp.float32)).astype(jnp.bfloat16)
    values = head_slice(val_tok, first_col)
    block_sum = jnp.einsum("gnm,ngd->mgd", upper, values, preferred_element_type=jnp.float32)
    block_sum = block_sum + jnp.einsum(
        "gnm,ngd->mgd", lower, values, preferred_element_type=jnp.float32
    )
    return (jnp.sum(exponent, axis=1), block_sum)


def per_device(
    tokens,
    latents,
    tok_gain,
    lat_gain,
    mlp_gain,
    w_ref_tok,
    w_val_tok,
    w_out_tok,
    w_ref_lat,
    w_val_lat,
    w_out_lat,
    w_up,
    w_down,
):
    ref_lat_w, val_lat_w, out_lat_w, up_full, down_full = (
        lax.all_gather(w_ref_lat, "member", axis=0, tiled=True),
        lax.all_gather(w_val_lat, "member", axis=0, tiled=True),
        lax.all_gather(w_out_lat, "member", axis=0, tiled=True),
        lax.all_gather(w_up, "member", axis=1, tiled=True),
        lax.all_gather(w_down, "member", axis=0, tiled=True),
    )
    lat_norm = (normalize(latents.astype(jnp.float32)) * lat_gain).astype(jnp.bfloat16)
    own_ref = project(lat_norm, ref_lat_w).astype(jnp.bfloat16)
    own_val = project(lat_norm, val_lat_w).astype(jnp.bfloat16)
    ref_lat, val_lat = (
        lax.all_gather(own_ref, "member", axis=0, tiled=True),
        lax.all_gather(own_val, "member", axis=0, tiled=True),
    )
    tok_norm = (normalize(tokens.astype(jnp.float32)) * tok_gain).astype(jnp.bfloat16)
    ref_tok = project(tok_norm, w_ref_tok).astype(jnp.bfloat16)
    val_tok = project(tok_norm, w_val_tok).astype(jnp.bfloat16)
    features = tokens.shape[1]
    lat_count = ref_lat.shape[0]
    block_width = BLOCK_HEADS * HEAD_DIM
    starts = list(range(0, features, block_width))
    tok_parts = []
    peaks = []
    for first_col in starts:
        attention_scores = head_scores(ref_tok, ref_lat, first_col)
        tok_parts.append(row_part(attention_scores, val_lat, first_col))
        peaks.append(jnp.max(attention_scores, axis=1))
    highest = lax.pmax(jnp.concatenate(peaks, 0).astype(jnp.bfloat16), ("group", "member")).astype(
        jnp.float32
    )
    totals = []
    sums_out = []
    for head_block, first_col in enumerate(starts):
        attention_scores = head_scores(ref_tok, ref_lat, first_col)
        shift = lax.slice_in_dim(
            highest, head_block * BLOCK_HEADS, (head_block + 1) * BLOCK_HEADS, axis=0
        )
        block_total, block_sum = column_part(attention_scores, shift, val_tok, first_col)
        totals.append(block_total)
        sums_out.append(block_sum)
    all_sums = jnp.concatenate(sums_out, 1).reshape(lat_count, features)
    all_totals = jnp.transpose(jnp.concatenate(totals, 0))
    share_sum, share_total = (
        lax.psum_scatter(all_sums, "member", scatter_dimension=0, tiled=True),
        lax.psum_scatter(all_totals, "member", scatter_dimension=0, tiled=True),
    )
    lat_sum, lat_total = lax.psum((share_sum, share_total), "group")
    lat_sum = lat_sum.reshape(lat_sum.shape[0], features // HEAD_DIM, HEAD_DIM)
    own_rows = lat_sum.shape[0]
    lat_attn = (lat_sum / lat_total[:, :, None]).reshape(own_rows, features)
    lat_mixed = normalize(lat_attn).astype(jnp.bfloat16)
    latents_out = (latents.astype(jnp.float32) + project(lat_mixed, out_lat_w)).astype(jnp.bfloat16)
    token_attention = jnp.concatenate(tok_parts, 1).astype(jnp.bfloat16)
    tok_mid = tokens.astype(jnp.float32) + project(token_attention, w_out_tok)
    mlp_in = (normalize(tok_mid) * mlp_gain).astype(jnp.bfloat16)
    hidden = jax.nn.gelu(project(mlp_in, up_full), approximate=False).astype(jnp.bfloat16)
    tokens_out = (tok_mid + project(hidden, down_full)).astype(jnp.bfloat16)
    return (tokens_out, latents_out)


def solution(mesh):
    in_specs = (
        P(("group", "member"), None),
        P("member", None),
        P(),
        P(),
        P(),
        P(),
        P(),
        P(),
        P("member", None),
        P("member", None),
        P("member", None),
        P(None, "member"),
        P("member", None),
    )
    out_specs = (P(("group", "member"), None), P("member", None))
    return jax.shard_map(
        per_device, mesh=mesh, in_specs=in_specs, out_specs=out_specs, check_vma=False
    )
```

profile of v0, /device:TPU:1, one launch (start us, length us, event | category | flops | bytes accessed | tf_op | source)
XLA Modules:
  0.0 606.3 jit_solution(17466379050091290530)
XLA Ops:
  8.0 1.0 fusion.78
  9.0 44.8 %all-gather.12.cloned.1.call-done = bf16[1024,1024]{1,0:T(8,128)(2,1)} async-done(((bf16[64,1024]{1,0:T(8,128)(2,1)}), bf16[1024,1024]{1,0:T(8,128)(2,1)}) %all-gather.12.cloned.1.call-update) | async-done | bytes 2097168 | tf_op jit(solution)/shard_map/all_gather | solution.py:74
  53.8 2.9 convolution_convert_fusion.2
  56.8 0.7 all-gather.8.cloned.1.call-update
  57.7 2.1 convolution_convert_fusion.1
  59.8 0.7 copy.61
  60.5 0.7 copy.58
  61.3 0.7 copy.55
  62.0 0.7 copy.52
  62.7 2.1 convolution_convert_fusion
  64.8 0.7 copy.66
  65.6 0.7 copy.65
  66.5 28.4 %all-gather.14.cloned.1.call-done = bf16[1024,1024]{1,0:T(8,128)(2,1)} async-done(((bf16[64,1024]{1,0:T(8,128)(2,1)}), bf16[1024,1024]{1,0:T(8,128)(2,1)}) %all-gather.14.cloned.1.call-update) | async-done | bytes 2097168 | tf_op jit(solution)/shard_map/all_gather | solution.py:84
  94.9 2.7 fusion.173
  97.6 2.1 copy.62
  99.7 1.0 copy.59
  100.9 1.2 copy.53
  102.2 3.0 multiply_reduce_fusion.2
  105.2 1.8 multiply_reduce_fusion
  106.9 1.8 multiply_reduce_fusion.4
  108.8 1.9 multiply_reduce_fusion.6
  111.3 76.9 %pmax.7 = bf16[16,1024]{1,0:T(8,128)(2,1)} all-reduce(bf16[16,1024]{1,0:T(8,128)(2,1)} %pad_maximum_fusion.1), channel_id=1, replica_groups=mesh['group'=16,'member'=16] {'group','member'}, use_global_device_ids=true, to_apply=%region_15.0 | all-reduce | flops 16384 | bytes 65536 | tf_op jit(solution)/shard_map/pmax | solution.py:100
  188.2 0.8 fusion.177
  189.0 3.8 fusion.16
  192.8 1.5 fusion.12
  196.1 1.0 copy-done.4
  197.0 0.7 fusion.8
  197.8 0.8 copy-done.2
  198.6 0.7 fusion.9
  199.4 0.7 fusion.10
  200.1 0.7 fusion.11
  200.8 2.5 pad_maximum_fusion
  203.3 5.3 copy.67
  208.8 0.8 copy-done.7
  209.6 2.8 convolution_convert_fusion.3
  213.0 0.7 all-gather.16.cloned.1.call-update
  213.7 1.4 maximum_bitcast_fusion
  215.1 1.8 copy.69
  217.0 47.9 %reduce-scatter.7.cloned.1.call-done = f32[64,1024]{1,0:T(8,128)} async-done(((f32[1024,1024]{1,0:T(8,128)}), f32[64,1024]{1,0:T(8,128)}) %reduce-scatter.7.cloned.1.call-update) | async-done | bytes 262160
  265.0 2.0 copy.68
  267.6 41.4 %all-gather.10.cloned.1.call-done = bf16[1024,1024]{1,0:T(8,128)(2,1)} async-done(((bf16[64,1024]{1,0:T(8,128)(2,1)}), bf16[1024,1024]{1,0:T(8,128)(2,1)}) %all-gather.10.cloned.1.call-update) | async-done | bytes 2097168 | tf_op jit(solution)/shard_map/all_gather | solution.py:85
  309.0 2.9 fusion.174
  311.8 2.1 copy.60
  313.9 2.1 copy.57
  316.0 2.0 copy.54
  318.0 2.1 copy.51
  320.1 1.9 fusion.178
  322.0 1.9 fusion.179
  323.9 1.7 fusion.180
  325.6 1.7 fusion.181
  327.3 2.9 convolution_convert_fusion.4
  330.2 2.9 convolution_convert_fusion.5
  333.0 2.7 convolution_convert_fusion.6
  335.7 2.1 convolution_convert_fusion.7
  338.4 12.7 %all-gather.18.cloned.1.call-done = bf16[2048,1024]{1,0:T(8,128)(2,1)} async-done(((bf16[128,1024]{1,0:T(8,128)(2,1)}), bf16[2048,1024]{1,0:T(8,128)(2,1)}) %all-gather.18.cloned.1.call-update) | async-done | bytes 4194320 | tf_op jit(solution)/shard_map/all_gather | solution.py:78
  351.1 49.8 %all-gather.16.cloned.1.call-done = bf16[1024,2048]{1,0:T(8,128)(2,1)} async-done(((bf16[1024,128]{1,0:T(8,128)(2,1)}), bf16[1024,2048]{1,0:T(8,128)(2,1)}) %all-gather.16.cloned.1.call-update) | async-done | bytes 4194320 | tf_op jit(solution)/shard_map/all_gather | solution.py:77
  400.9 7.8 %fusion.20 = bf16[128,1024]{1,0:T(8,128)(2,1)} fusion(f32[128,1024]{1,0:T(8,128)S(1)} %get-tuple-element.33, bf16[2048,1024]{1,0:T(8,128)(2,1)} %all-gather.18.cloned.1.call-done, bf16[1024,2048]{1,0:T(8,128)(2,1)} %all-gather.16.cloned.1.call-done, f32[1024]{0:T(1024)S(1)} %copy-done.18, f32[128]{0:T(128)S(1)} %add_rsqrt_fusion.1), kind=kOutput, calls=%fused_computation.54 | convolution fusion | flops 1091436544 | bytes 9179648 | tf_op jit(solution)/shard_map/dot_general | solution.py:18
  408.6 46.5 %reduce-scatter.9.cloned.1.call-done = f32[64,16]{1,0:T(8,128)} async-done(((f32[1024,16]{1,0:T(8,128)}), f32[64,16]{1,0:T(8,128)}) %reduce-scatter.9.cloned.1.call-update) | async-done | bytes 4112
  455.1 0.8 copy.70
  455.9 33.7 %psum.15 = f32[64,16]{0,1:T(8,128)S(1)} all-reduce(f32[64,16]{0,1:T(8,128)S(1)} %copy.70), channel_id=1, replica_groups=mesh['group'=16,'member'=16] {'group'}, use_global_device_ids=true, to_apply=%region_23.0 | all-reduce | flops 1024 | bytes 8192 | tf_op jit(solution)/shard_map/psum | solution.py:119
  489.6 64.5 %all-reduce.2.cloned.1.call-done = f32[64,1024]{0,1:T(8,128)} async-done(((f32[64,1024]{0,1:T(8,128)}), f32[64,1024]{0,1:T(8,128)}) %all-reduce.2.cloned.1.call-update) | async-done | bytes 262160 | tf_op jit(solution)/shard_map/psum | solution.py:119
  554.1 1.2 multiply_reduce_fusion.8
  555.3 41.4 %all-gather.20.cloned.1.call-done = bf16[1024,1024]{1,0:T(8,128)(2,1)} async-done(((bf16[64,1024]{1,0:T(8,128)(2,1)}), bf16[1024,1024]{1,0:T(8,128)(2,1)}) %all-gather.20.cloned.1.call-update) | async-done | bytes 2097168 | tf_op jit(solution)/shard_map/all_gather | solution.py:76
  596.7 2.8 fusion.21
  (70 shorter events, 5.9 us)
Async XLA Ops:
  7.2 330.6 %copy-start = (bf16[1024,1024]{1,0:T(8,128)(2,1)S(1)}, bf16[1024,1024]{1,0:T(8,128)(2,1)}, u32[]{:S(2)}) copy-start(bf16[1024,1024]{1,0:T(8,128)(2,1)} %param.20) | copy-start | bytes 6291460
  7.2 50.3 %copy-start.5 = (bf16[128,1024]{1,0:T(8,128)(2,1)S(1)}, bf16[128,1024]{1,0:T(8,128)(2,1)}, u32[]{:S(2)}) copy-start(bf16[128,1024]{1,0:T(8,128)(2,1)} %param.13) | copy-start | bytes 786436
  7.2 50.5 %copy-start.16 = (f32[1024]{0:T(1024)S(1)}, f32[1024]{0:T(1024)}, u32[]{:S(2)}) copy-start(f32[1024]{0:T(1024)} %param.15) | copy-start | bytes 12292
  7.2 46.6 %all-gather.12.cloned.1.call-start = ((), (), s32[]{:S(2)}) async-start(), calls=%async_computation.4 | async-start | bytes 2228224 | tf_op jit(solution)/shard_map/all_gather | solution.py:74
  7.9 87.0 %all-gather.14.cloned.1.call-start = ((), (), s32[]{:S(2)}) async-start(), calls=%async_computation.5 | async-start | bytes 2228224 | tf_op jit(solution)/shard_map/all_gather | solution.py:84
  9.0 48.6 %copy-start.17 = (f32[64]{0:T(128)}, f32[64]{0:T(128)S(1)}, u32[]{:S(2)}) copy-start(f32[64]{0:T(128)S(1)} %add_rsqrt_fusion.3) | copy-start | bytes 772
  56.7 152.0 %all-gather.8.cloned.1.call-start = ((), (), s32[]{:S(2)}) async-start(), calls=%async_computation.2 | async-start | bytes 2228224 | tf_op jit(solution)/shard_map/all_gather | solution.py:75
  57.5 207.5 %reduce-scatter.7.cloned.1.call-start = ((), (), s32[]{:S(2)}) async-start(), calls=%async_computation.10 | async-start | bytes 4456448
  102.1 3.0 copy-start.6
  102.1 3.0 copy-start.12
  102.2 4.8 copy-start.11
  105.2 3.6 copy-start.10
  189.0 3.8 copy-start.1
  189.0 3.8 copy-start.3
  192.8 1.5 copy-start.9
  194.3 0.8 copy-start.8
  195.5 1.6 copy-start.4
  197.0 1.6 copy-start.2
  208.6 0.9 copy-start.7
  208.7 100.3 %all-gather.10.cloned.1.call-start = ((), (), s32[]{:S(2)}) async-start(), calls=%async_computation.3 | async-start | bytes 2228224 | tf_op jit(solution)/shard_map/all_gather | solution.py:85
  212.4 138.7 %all-gather.18.cloned.1.call-start = ((), (), s32[]{:S(2)}) async-start(), calls=%async_computation.7 | async-start | bytes 4456448 | tf_op jit(solution)/shard_map/all_gather | solution.py:78
  212.9 187.9 %all-gather.16.cloned.1.call-start = ((), (), s32[]{:S(2)}) async-start(), calls=%async_computation.6 | async-start | bytes 4456448 | tf_op jit(solution)/shard_map/all_gather | solution.py:77
  213.7 241.4 %reduce-scatter.9.cloned.1.call-start = ((), (), s32[]{:S(2)}) async-start(), calls=%async_computation.11 | async-start | bytes 557056
  217.0 337.1 %all-reduce.2.cloned.1.call-start = ((), (), s32[]{:S(2)}) async-start(), calls=%async_computation.8 | async-start | bytes 1048576 | tf_op jit(solution)/shard_map/psum | solution.py:119
  267.0 329.7 %all-gather.20.cloned.1.call-start = ((), (), s32[]{:S(2)}) async-start(), calls=%async_computation.9 | async-start | bytes 2228224 | tf_op jit(solution)/shard_map/all_gather | solution.py:76
  335.7 2.1 copy-start.13
  335.7 2.1 copy-start.14
  335.7 2.1 copy-start.15
  337.8 63.1 %copy-start.18 = (f32[1024]{0:T(1024)S(1)}, f32[1024]{0:T(1024)}, u32[]{:S(2)}) copy-start(f32[1024]{0:T(1024)} %param.17) | copy-start | bytes 12292
Sparse Core Ops, SparseCore 0:
  9.9 43.9 all-gather.11
  56.9 38.0 all-gather.13
  96.8 38.0 all-gather.7
  208.8 56.1 reduce-scatter.6
  267.2 41.7 all-gather.9
  310.7 40.3 all-gather.17
  352.8 47.9 all-gather.15
  403.3 51.7 reduce-scatter.8
  458.6 95.4 all-reduce.1
  555.8 40.8 all-gather.19
where the time goes:
time: 608 us; the launch traced here: 606 us
  waiting for transfers between devices  380 us (62%)
  blocking collectives  111 us (18%)
  matrix products  51.1 us (8%)
  local copies, waits for them, and re-layouts  36.9 us (6%)
  between operations  14.5 us (2%)
  other arithmetic  12.2 us (2%)
    unnamed x12, waiting for transfers between devices  97.4 us
    pmax x1, blocking collectives, per_device(): lax.pmax(jnp.concatenate(peaks, 0).astype(jnp.bfloat16), ('group', 'membe...  76.9 us
    psum x1, waiting for transfers between devices, per_device(): lat_sum, lat_total = lax.psum((share_sum, share_total), 'group')  64.5 us
    all_gather x1, waiting for transfers between devices, per_device(): lax.all_gather(w_up, 'member', axis=1, tiled=True)  49.8 us
    all_gather x1, waiting for transfers between devices, per_device(): lax.all_gather(w_ref_lat, 'member', axis=0, tiled=True)  44.8 us
    all_gather x1, waiting for transfers between devices, per_device(): lax.all_gather(own_val, 'member', axis=0, tiled=True)  41.4 us
    all_gather x1, waiting for transfers between devices, per_device(): lax.all_gather(w_out_lat, 'member', axis=0, tiled=True)  41.4 us
    psum x1, blocking collectives, per_device(): lat_sum, lat_total = lax.psum((share_sum, share_total), 'group')  33.7 us
  transfers between devices with their start and end apart: 10, of which 9 were waited for; matrix products, arithmetic and copies ran while one was open for 15% of the time, Pallas kernels for 0%

commit v1 on v0

v1 whole, which is shorter than its diff:
```python
import functools

import jax
import jax.numpy as jnp
from jax import lax
from jax.experimental import pallas as pl
from jax.experimental.pallas import tpu as pltpu
from jax.sharding import PartitionSpec as P

HEAD_DIM = 64
PAIR = 2 * HEAD_DIM
NORM_EPS = 1e-06
MESH = pl.DeviceIdType.MESH
F32 = jnp.float32
BF16 = jnp.bfloat16

(
    S_W, S_LAT, S_UP1, S_DOWN1, S_WOUT, S_PROJ, S_PROJ2, S_UP2, S_DOWN2, S_UP3, S_DOWN3,
    S_ATT, S_COL, S_RS, S_ZC, S_AG, S_SQ, S_PART, S_LO, S_MIN, S_MP0, S_MP1, S_RV,
) = range(23)


def scale_of(values):
    return lax.rsqrt(jnp.mean(values * values, axis=-1, keepdims=True) + NORM_EPS)


def dot(left_side, right_side):
    return jnp.dot(left_side, right_side, preferred_element_type=F32)


def gelu(values):
    return 0.5 * values * (1.0 + lax.erf(values * (0.5**0.5)))


def kernel(
    nx, ny, nz,
    tokens, latents, tok_gain, lat_gain, mlp_gain,
    w_ref_tok, w_val_tok, w_out_tok, w_ref_lat, w_val_lat, w_out_lat, w_up, w_down,
    tokens_out, latents_out,
    wtok, up, down, wlat, latx, wout, rvo, rv, lat_rv, km, vm, scores, cmax, acc, att_out, att,
    col_in, blk, rs, zb, lab, sq, sq_in, part, part_in, mid, mlp_in, hid, mp, mp_in,
    load, send, recv,
):
    ng = nx * ny
    nm = 2 * nz
    rows, width = tokens.shape
    g = lax.axis_index("group")
    m = lax.axis_index("member")
    z = lax.div(m, 2)
    c = lax.rem(m, 2)
    y = lax.div(g, nx)
    x = lax.rem(g, nx)
    other = 1 - c
    partner = (g, z * 2 + other)
    gpair = lax.div(g, 2)

    def remote(src, dst, slot, device):
        return pltpu.make_async_remote_copy(
            src_ref=src, dst_ref=dst, send_sem=send.at[min(slot, S_RV)] if isinstance(slot, int) else send.at[S_RV],
            recv_sem=recv.at[slot], device_id=device, device_id_type=MESH,
        )

    def local(src, dst, slot):
        return pltpu.make_async_copy(src, dst, recv.at[slot])

    def wait_recv(ref, slot):
        pltpu.make_async_copy(ref, ref, recv.at[slot]).wait()

    def wait_send(ref, slot):
        pltpu.make_async_copy(ref, ref, send.at[slot]).wait()

    def each(low, high, body):
        def step(i, carry):
            body(i)
            return carry

        lax.fori_loop(low, high, step, 0)

    def lanes(index, size=PAIR):
        return pl.ds(pl.multiple_of(index * size, size), size)

    def block_rows(index, size=64):
        return pl.ds(pl.multiple_of(index * size, size), size)

    loads = [
        pltpu.make_async_copy(w_ref_tok, wtok.at[0], load.at[0]),
        pltpu.make_async_copy(w_val_tok, wtok.at[1], load.at[1]),
        pltpu.make_async_copy(w_out_tok, wtok.at[2], load.at[2]),
        pltpu.make_async_copy(w_up, up.at[0], load.at[3]),
        pltpu.make_async_copy(w_down, down.at[0], load.at[4]),
    ]
    for item in loads:
        item.start()

    barrier = pltpu.get_barrier_semaphore()

    def greet(device):
        pl.semaphore_signal(barrier, inc=1, device_id=device, device_id_type=MESH)

    each(1, nm, lambda k: greet((g, lax.rem(m + k, nm))))
    each(1, ng, lambda k: greet((lax.rem(g + k, ng), m)))

    @pl.when(g != m)
    def _():
        greet((m, g))

    pl.semaphore_wait(barrier, nm + ng - 2 + (g != m).astype(jnp.int32))

    own_rows = block_rows(m)

    def send_w(k):
        zz = lax.rem(z + k, nz)
        remote(w_ref_lat.at[:, lanes(zz)], wlat.at[own_rows, :], S_W, (g, zz * 2)).start()
        remote(w_val_lat.at[:, lanes(zz)], wlat.at[own_rows, :], S_W, (g, zz * 2 + 1)).start()

    @pl.when(g != m)
    def _():
        remote(latents, latx, S_LAT, (m, g)).start()

    @pl.when(g == m)
    def _():
        local(latents, latx, S_LAT).start()

    each(1, nz, send_w)

    @pl.when(c == 0)
    def _():
        local(w_ref_lat.at[:, lanes(z)], wlat.at[own_rows, :], S_W).start()
        remote(w_val_lat.at[:, lanes(z)], wlat.at[own_rows, :], S_W, partner).start()

    @pl.when(c == 1)
    def _():
        local(w_val_lat.at[:, lanes(z)], wlat.at[own_rows, :], S_W).start()
        remote(w_ref_lat.at[:, lanes(z)], wlat.at[own_rows, :], S_W, partner).start()

    up_rows = width // ng
    down_rows = down.shape[1] // ny
    down_cols = width // nx
    up_piece = block_rows(g, up_rows)
    down_piece = (block_rows(y, down_rows), lanes(x, down_cols))

    def send_mlp(k):
        device = (g, lax.rem(z + k, nz) * 2 + c)
        remote(w_up.at[up_piece, :], up.at[nz - k, up_piece, :], S_UP1, device).start()
        remote(
            w_down.at[down_piece[0], down_piece[1]],
            down.at[nz - k, down_piece[0], down_piece[1]], S_DOWN1, device,
        ).start()

    each(1, nz, send_mlp)

    tok32 = tokens[...].astype(F32)
    tok_norm = (tok32 * scale_of(tok32) * tok_gain[...]).astype(BF16)
    loads[0].wait()
    loads[1].wait()
    for kind in range(2):
        for n in range(nz // 2):
            made = dot(tok_norm, wtok[kind, :, n * 256 : (n + 1) * 256]).astype(BF16)
            for i in range(2):
                rvo[2 * n + i, :, kind * PAIR : (kind + 1) * PAIR] = made[:, i * PAIR : (i + 1) * PAIR]
    local(rvo.at[z], rv.at[0], S_RV).start()

    def send_rv(k):
        zz = lax.rem(z + k, nz)
        remote(rvo.at[zz], rv.at[nz - k], S_RV + nz - k, (g, zz * 2 + c)).start()

    each(1, nz, send_rv)

    def send_wout(k):
        device = (g, lax.rem(z + k, nz) * 2 + c)
        remote(w_out_lat.at[:, lanes(gpair)], wout.at[block_rows(k), :], S_WOUT, device).start()

    local(w_out_lat.at[:, lanes(gpair)], wout.at[pl.ds(0, 64), :], S_WOUT).start()
    each(1, nz, send_wout)

    wait_recv(latx, S_LAT)
    lat32 = latx[...].astype(F32)
    lat_norm = (lat32 * scale_of(lat32) * lat_gain[...]).astype(BF16)
    wait_recv(wlat, S_W)
    proj_rows = block_rows(g)
    lat_rv[c, proj_rows, :] = dot(lat_norm, wlat[...]).astype(BF16)

    def send_proj(k):
        block = lat_rv.at[c, proj_rows, :]
        remote(block, block, S_PROJ, (lax.rem(g + k, ng), m)).start()

    each(1, ng, send_proj)

    wait_recv(up.at[pl.ds(1, nz - 1), up_piece, :], S_UP1)
    wait_recv(down.at[pl.ds(1, nz - 1), down_piece[0], down_piece[1]], S_DOWN1)

    def x_peer(k):
        return (y * nx + lax.rem(x + k, nx), m)

    def y_peer(k):
        return (lax.rem(y + k, ny) * nx + x, m)

    def send_up2(k):
        block = up.at[pl.ds(1, nz - 1), up_piece, :]
        remote(block, block, S_UP2, x_peer(k)).start()

    def send_down2(k):
        block = down.at[pl.ds(1, nz - 1), down_piece[0], down_piece[1]]
        remote(block, block, S_DOWN2, y_peer(k)).start()

    each(1, nx, send_up2)
    each(1, ny, send_down2)

    wait_recv(lat_rv.at[0, pl.ds(0, (ng - 1) * 64), :], S_PROJ)
    remote(lat_rv.at[c], lat_rv.at[c], S_PROJ2, partner).start()

    wait_recv(up.at[pl.ds(1, nz - 1), pl.ds(0, (nx - 1) * up_rows), :], S_UP2)
    wait_recv(down.at[pl.ds(1, nz - 1), pl.ds(0, (ny - 1) * down_rows), pl.ds(0, down_cols)], S_DOWN2)
    up_wide = block_rows(y, nx * up_rows)

    def send_up3(k):
        block = up.at[pl.ds(1, nz - 1), up_wide, :]
        remote(block, block, S_UP3, y_peer(k)).start()

    def send_down3(k):
        block = down.at[pl.ds(1, nz - 1), :, down_piece[1]]
        remote(block, block, S_DOWN3, x_peer(k)).start()

    each(1, ny, send_up3)
    each(1, nx, send_down3)

    wait_recv(lat_rv.at[other], S_PROJ2)
    lat_count = lat_rv.shape[1]
    lane = lax.broadcasted_iota(jnp.int32, (lat_count, PAIR), 1)
    keys = lat_rv[0].astype(F32) * HEAD_DIM ** (-0.5)
    values = lat_rv[1].astype(F32)
    for h in range(2):
        mine = (lane < HEAD_DIM) if h == 0 else (lane >= HEAD_DIM)
        km[h] = jnp.where(mine, keys, 0.0).astype(BF16)
        vm[h] = jnp.where(mine, values, 0.0).astype(BF16)

    cmax[...] = jnp.full(cmax.shape, -jnp.inf, F32)
    pair_lanes = lanes(z)

    def attend(i):
        half = lax.div(i + 1, 2)
        k = jnp.where(lax.rem(i, 2) == 1, half, lax.rem(nz - half, nz))
        wait_recv(rv.at[k], S_RV + k)
        query = rv[k, :, 0:PAIR]
        result = jnp.zeros((rows, PAIR), F32)
        for h in range(2):
            score = lax.dot_general(query, km[h], (((1,), (1,)), ((), ())), preferred_element_type=F32)
            scores[h, k] = score
            cmax[h] = jnp.maximum(cmax[h], jnp.max(score.reshape(rows // 8, 8, lat_count), axis=0))
            exponent = jnp.exp(score - jnp.max(score, axis=1, keepdims=True))
            inverse = 1.0 / jnp.sum(exponent, axis=1, keepdims=True)
            result = result + dot((exponent * inverse).astype(BF16), vm[h])
        att_out[k] = result.astype(BF16)

        @pl.when(i == 0)
        def _():
            local(att_out.at[0], att.at[:, pair_lanes], S_ATT).start()

        @pl.when(i > 0)
        def _():
            device = (g, lax.rem(z + k, nz) * 2 + c)
            remote(att_out.at[k], att.at[:, pair_lanes], S_ATT, device).start()

    each(0, nz, attend)

    peaks = [jnp.max(cmax[h], axis=0, keepdims=True) for h in range(2)]
    acc[...] = jnp.zeros(acc.shape, F32)

    def columns(t):
        pair = rv[pl.ds(2 * t, 2), :, PAIR : 2 * PAIR].reshape(2 * rows, PAIR)
        turned = pair.astype(F32).T.astype(BF16)
        ones = jnp.ones((16, 2 * rows), BF16)
        for h in range(2):
            score = scores[h, pl.ds(2 * t, 2)].reshape(2 * rows, lat_count)
            exponent = jnp.exp(score - peaks[h]).astype(BF16)
            left = jnp.concatenate([turned[h * HEAD_DIM : (h + 1) * HEAD_DIM], ones], axis=0)
            acc[h] = acc[h] + dot(left, exponent)

    each(0, nz // 2, columns)
    for h in range(2):
        acc[h, 72:80, :] = jnp.broadcast_to(peaks[h], (8, lat_count))
    remote(acc.at[other], col_in, S_COL, partner).start()

    wait_recv(att, S_ATT)
    loads[2].wait()
    mid[...] = tokens[...].astype(F32) + dot(att[...], wtok[2])
    mid32 = mid[...]
    mlp_in[c] = (mid32 * scale_of(mid32) * mlp_gain[...]).astype(BF16)
    remote(mlp_in.at[c], mlp_in.at[c], S_MIN, partner).start()

    wait_recv(col_in, S_COL)
    own_peak = acc[c, 72:80, :]
    in_peak = col_in[72:80, :]
    peak = jnp.maximum(own_peak, in_peak)
    own_scale = jnp.exp(own_peak - peak)
    in_scale = jnp.exp(in_peak - peak)
    own_sums = acc[c, 0:72, :].reshape(9, 8, lat_count)
    in_sums = col_in[0:72, :].reshape(9, 8, lat_count)
    sums = (own_sums * own_scale[None] + in_sums * in_scale[None]).reshape(72, lat_count)
    for b in range(ng):
        span = slice((b // 2) * PAIR, (b // 2 + 1) * PAIR)
        blk[b, 0:32, :] = sums[(b % 2) * 32 : (b % 2) * 32 + 32, span]
        blk[b, 32:40, :] = sums[64:72, span]
        blk[b, 40:48, :] = peak[:, span]

    def block_of(gg):
        return 2 * lax.rem(z + lax.div(gg, 2), nz) + lax.rem(gg, 2)

    def send_blk(k):
        gg = lax.rem(g + k, ng)
        remote(blk.at[block_of(gg)], rs.at[g], S_RS, (gg, m)).start()

    local(blk.at[block_of(g)], rs.at[g], S_RS).start()
    each(1, ng, send_blk)

    loads[3].wait()
    loads[4].wait()
    wait_recv(mlp_in.at[other], S_MIN)
    wait_recv(up.at[pl.ds(1, nz - 1), pl.ds(0, (ny - 1) * nx * up_rows), :], S_UP3)
    both = mlp_in[...].reshape(2 * rows, width)
    for n in range(nz // 2):
        piece = jnp.concatenate([up[2 * n], up[2 * n + 1]], axis=1)
        hid[:, n * 256 : (n + 1) * 256] = gelu(dot(both, piece)).astype(BF16)

    wait_recv(rs, S_RS)
    all_peaks = rs[:, 40:48, :]
    factor = jnp.exp(all_peaks - jnp.max(all_peaks, axis=0, keepdims=True))
    total = jnp.sum(rs[:, 32:40, :] * factor, axis=0)
    summed = jnp.sum(rs[:, 0:32, :].reshape(ng, 4, 8, PAIR) * factor[:, None], axis=0)
    zb[...] = (summed / total[None]).reshape(32, PAIR)
    owner = lax.rem(z + gpair, nz)

    @pl.when(owner == z)
    def _():
        local(zb, lab.at[g], S_ZC).start()

    @pl.when(owner != z)
    def _():
        remote(zb, lab.at[g], S_ZC, (g, owner * 2 + c)).start()

    wait_recv(down.at[pl.ds(1, nz - 1), :, pl.ds(0, (nx - 1) * down_cols)], S_DOWN3)
    hidden = hid[...]
    half_width = width // 2

    def mlp_out(first, last, slot):
        for n in range(first, last, min(256, half_width)):
            span = slice(n, n + min(256, half_width))
            made = dot(hidden, down[:, :, span].reshape(hidden.shape[1], min(256, half_width)))
            mp[:, :, span] = made.reshape(2, rows, min(256, half_width))
        span = pl.ds(first, last - first)
        remote(mp.at[other, :, span], mp_in.at[:, span], slot, partner).start()

    mlp_out(0, half_width, S_MP0)

    wait_recv(zb, S_ZC)

    def send_lab(k):
        remote(lab.at[g], lab.at[g], S_AG, (lax.rem(g + k, ng), m)).start()

    each(1, ng, send_lab)

    mlp_out(half_width, width, S_MP1)

    wait_recv(lab.at[pl.ds(0, ng - 1)], S_AG)
    attended = lab[...].reshape(ng * 32, PAIR)
    sq[...] = jnp.broadcast_to(jnp.sum(attended * attended, axis=0, keepdims=True), (8, PAIR))
    remote(sq, sq_in, S_SQ, partner).start()

    wait_recv(mp_in.at[:, pl.ds(0, half_width)], S_MP0)
    tokens_out[:, 0:half_width] = (
        mid[:, 0:half_width] + (mp[c, :, 0:half_width] + mp_in[:, 0:half_width])
    ).astype(BF16)

    wait_recv(sq_in, S_SQ)
    norm = lax.rsqrt((sq[0:1, :] + sq_in[0:1, :]) * (1.0 / width) + NORM_EPS)
    mixed = (attended * norm).T.astype(BF16)
    wait_recv(wout, S_WOUT)
    part[...] = dot(mixed, wout[...]).reshape(2, 64, PAIR)
    remote(part.at[other], part_in, S_PART, partner).start()

    wait_recv(mp_in.at[:, pl.ds(half_width, half_width)], S_MP1)
    tokens_out[:, half_width:width] = (
        mid[:, half_width:width] + (mp[c, :, half_width:width] + mp_in[:, half_width:width])
    ).astype(BF16)

    wait_recv(part_in, S_PART)
    own_lanes = lanes(gpair)
    latents_out[:, own_lanes] = (
        latents[:, own_lanes].astype(F32) + (part[c] + part_in[...])
    ).astype(BF16)

    def send_lo(k):
        device = (2 * lax.rem(gpair + k, nz) + lax.rem(g, 2), m)
        remote(latents_out.at[:, own_lanes], latents_out.at[:, own_lanes], S_LO, device).start()

    each(1, nz, send_lo)
    wait_recv(latents_out.at[:, pl.ds(0, (nz - 1) * PAIR)], S_LO)

    @pl.when(g != m)
    def _():
        wait_send(latx, S_LAT)

    @pl.when(owner != z)
    def _():
        wait_send(zb, S_ZC)

    wait_send(wlat.at[pl.ds(0, (nm - 1) * 64), :], S_W)
    wait_send(up.at[pl.ds(1, nz - 1), up_piece, :], S_UP1)
    wait_send(down.at[pl.ds(1, nz - 1), down_piece[0], down_piece[1]], S_DOWN1)
    wait_send(rv.at[pl.ds(1, nz - 1)], S_RV)
    wait_send(wout.at[pl.ds(0, (nz - 1) * 64), :], S_WOUT)
    wait_send(lat_rv.at[0, pl.ds(0, (ng - 1) * 64), :], S_PROJ)
    wait_send(lat_rv.at[0], S_PROJ2)
    wait_send(up.at[pl.ds(1, nz - 1), pl.ds(0, (nx - 1) * up_rows), :], S_UP2)
    wait_send(down.at[pl.ds(1, nz - 1), pl.ds(0, (ny - 1) * down_rows), pl.ds(0, down_cols)], S_DOWN2)
    wait_send(up.at[pl.ds(1, nz - 1), pl.ds(0, (ny - 1) * nx * up_rows), :], S_UP3)
    wait_send(down.at[pl.ds(1, nz - 1), :, pl.ds(0, (nx - 1) * down_cols)], S_DOWN3)
    wait_send(att_out.at[pl.ds(1, nz - 1)], S_ATT)
    wait_send(col_in, S_COL)
    wait_send(mlp_in.at[0], S_MIN)
    wait_send(rs.at[pl.ds(0, ng - 1)], S_RS)
    wait_send(lab.at[pl.ds(0, ng - 1)], S_AG)
    wait_send(sq_in, S_SQ)
    wait_send(part_in, S_PART)
    wait_send(mp_in.at[:, pl.ds(0, half_width)], S_MP0)
    wait_send(mp_in.at[:, pl.ds(half_width, half_width)], S_MP1)
    wait_send(latents_out.at[:, pl.ds(0, (nz - 1) * PAIR)], S_LO)


def per_device(nx, ny, nz, *args):
    (tokens, latents, tok_gain, lat_gain, mlp_gain, *weights) = args
    ng = nx * ny
    rows, width = tokens.shape
    lat_count = latents.shape[0] * 2 * nz
    unit = weights[6].shape[1]
    vmem = pl.BlockSpec(memory_space=pltpu.VMEM)
    anywhere = pl.BlockSpec(memory_space=pl.ANY)
    scratch = [
        ((3, width, width), BF16),
        ((nz, width, unit), BF16),
        ((nz, unit, width), BF16),
        ((width, PAIR), BF16),
        ((64, width), BF16),
        ((nz * 64, PAIR), BF16),
        ((nz, rows, 2 * PAIR), BF16),
        ((nz, rows, 2 * PAIR), BF16),
        ((2, lat_count, PAIR), BF16),
        ((2, lat_count, PAIR), BF16),
        ((2, lat_count, PAIR), BF16),
        ((2, nz, rows, lat_count), F32),
        ((2, 8, lat_count), F32),
        ((2, 80, lat_count), F32),
        ((nz, rows, PAIR), BF16),
        ((rows, width), BF16),
        ((80, lat_count), F32),
        ((ng, 48, PAIR), F32),
        ((ng, 48, PAIR), F32),
        ((32, PAIR), F32),
        ((ng, 32, PAIR), F32),
        ((8, PAIR), F32),
        ((8, PAIR), F32),
        ((2, 64, PAIR), F32),
        ((64, PAIR), F32),
        ((rows, width), F32),
        ((2, rows, width), BF16),
        ((2 * rows, nz * unit), BF16),
        ((2, rows, width), F32),
        ((rows, width), F32),
    ]
    return pl.pallas_call(
        functools.partial(kernel, nx, ny, nz),
        out_shape=(
            jax.ShapeDtypeStruct(tokens.shape, BF16),
            jax.ShapeDtypeStruct(latents.shape, BF16),
        ),
        in_specs=[vmem] * 5 + [anywhere] * 8,
        out_specs=(vmem, vmem),
        scratch_shapes=[pltpu.VMEM(shape, kind) for shape, kind in scratch]
        + [
            pltpu.SemaphoreType.DMA((5,)),
            pltpu.SemaphoreType.DMA((S_RV + 1,)),
            pltpu.SemaphoreType.DMA((S_RV + nz,)),
        ],
        compiler_params=pltpu.CompilerParams(
            collective_id=0, has_side_effects=True, vmem_limit_bytes=56 * 1024 * 1024
        ),
        name="layer",
    )(
        tokens,
        latents,
        tok_gain.reshape(1, width),
        lat_gain.reshape(1, width),
        mlp_gain.reshape(1, width),
        *weights,
    )


def solution(mesh):
    ng = mesh.shape["group"]
    nz = mesh.shape["member"] // 2
    nx = int(round(ng**0.5))
    in_specs = (
        P(("group", "member"), None),
        P("member", None),
        P(),
        P(),
        P(),
        P(),
        P(),
        P(),
        P("member", None),
        P("member", None),
        P("member", None),
        P(None, "member"),
        P("member", None),
    )
    out_specs = (P(("group", "member"), None), P("member", None))
    return jax.shard_map(
        functools.partial(per_device, nx, ng // nx, nz),
        mesh=mesh, in_specs=in_specs, out_specs=out_specs, check_vma=False,
    )
```

time: 608 us -> 97 us (0.16)
  waiting for transfers between devices: 380 us -> 0 us
  blocking collectives: 111 us -> 0 us
  Pallas kernels: 0 us -> 92.1 us
  matrix products: 51.1 us -> 0 us
  local copies, waits for them, and re-layouts: 36.9 us -> 3.24 us
  between operations: 14.5 us -> 0.64 us
  other arithmetic: 12.2 us -> 0 us
    all_gather x7 -> x0, waiting for transfers between devices: 219 us -> none  [the longest x1 49.8 us: per_device(): lax.all_gather(w_up, 'member', axis=1, tiled=True)]
    unnamed x12 -> x0, waiting for transfers between devices: 97.4 us -> none
    pallas_call x0 -> x1, Pallas kernels: none -> 92.1 us  [per_device(): pl.pallas_call(functools.partial(kernel, nx, ny, nz), out_shape=(jax.Shap...]
    pmax x1 -> x0, blocking collectives: 76.9 us -> none  [per_device(): lax.pmax(jnp.concatenate(peaks, 0).astype(jnp.bfloat16), ('group', 'membe...]
    psum x1 -> x0, waiting for transfers between devices: 64.5 us -> none  [per_device(): lat_sum, lat_total = lax.psum((share_sum, share_total), 'group')]
    dot_general x23 -> x0, matrix products: 43.9 us -> none  [the longest x7 20.9 us: project(): return jnp.dot(left_side, right_side, preferred_element_type=jnp.float32)]
    psum x1 -> x0, blocking collectives: 33.7 us -> none  [per_device(): lat_sum, lat_total = lax.psum((share_sum, share_total), 'group')]
    slice x21 -> x0, local copies, waits for them, and re-layouts: 23.7 us -> none  [the longest x20 22.9 us: head_slice(): lax.slice_in_dim(matrix, first_col, first_col + BLOCK_HEADS * HEAD_DIM, a...]
  transfers between devices with their start and end apart: 10 -> 0, of which waited for: 9 -> 0; matrix products, arithmetic and copies ran while one was open for 15% -> 0% of each run, Pallas kernels for 0% -> 0%
where the time goes in v1:
time: 97 us; the launch traced here: 96 us
  Pallas kernels  92.1 us (95%)
  local copies, waits for them, and re-layouts  3.24 us (3%)
    pallas_call x1, Pallas kernels, per_device(): pl.pallas_call(functools.partial(kernel, nx, ny, nz), out_shape=(jax.Shap...  92.1 us
    unnamed x2, local copies, waits for them, and re-layouts  3.24 us

profile of v1, /device:TPU:1, one launch (start us, length us, event | category | flops | bytes accessed | tf_op | source)
XLA Modules:
  0.0 96.0 jit_solution(12658277327494024435)
XLA Ops:
  0.6 92.1 %layer.1 = (bf16[128,1024]{1,0:T(8,128)(2,1)}, bf16[64,1024]{1,0:T(8,128)(2,1)}) custom-call(bf16[128,1024]{1,0:T(8,128)(2,1)} %tokens.1, bf16[64,1024]{1,0:T(8,128)(2,1)} %latents.1, f32[1,1024]{1,0:T(1,128)} %bitcast.3, f32[1,1024]{1,0:T(1,128)} %bitcast.4, f32[1,1024]{1,0:T(1,128)} %bitcast.5, bf16[1024,1024]{1,0:T(8,128)(2,1)} %w_ref_tok.1, ...), custom_call_target="tpu_custom_call" | custom-call | tf_op jit(solution)/shard_map/layer/pallas_call | solution.py:470
  92.8 1.7 %copy.17 = bf16[128,1024]{1,0:T(8,128)(2,1)} copy(bf16[128,1024]{1,0:T(8,128)(2,1)} %get-tuple-element.4) | data formatting | bytes 524288
  94.5 1.6 %copy.18 = bf16[64,1024]{1,0:T(8,128)(2,1)} copy(bf16[64,1024]{1,0:T(8,128)(2,1)} %get-tuple-element.5) | data formatting | bytes 262144

commit v2 on v1

v2 whole, which is shorter than its diff:
```python
import functools

import jax
import jax.numpy as jnp
from jax import lax
from jax.experimental import pallas as pl
from jax.experimental.pallas import tpu as pltpu
from jax.sharding import PartitionSpec as P

HEAD_DIM = 64
PAIR = 2 * HEAD_DIM
NORM_EPS = 1e-06
MESH = pl.DeviceIdType.MESH
F32 = jnp.float32
BF16 = jnp.bfloat16

(
    S_W, S_W2, S_LAT, S_UP1, S_DOWN1, S_WOUT, S_VAL, S_PROJ, S_PROJ2, S_ATT, S_COL, S_RS, S_ZC, S_AG,
    S_SQ, S_PART, S_LO, S_MIN, S_MP0, S_MP1,
) = range(20)
S_RING = 20
S_REF = 36


def scale_of(values):
    return lax.rsqrt(jnp.mean(values * values, axis=-1, keepdims=True) + NORM_EPS)


def dot(left_side, right_side):
    return jnp.dot(left_side, right_side, preferred_element_type=F32)


def gelu(values):
    return 0.5 * values * (1.0 + lax.erf(values * (0.5**0.5)))


def kernel(
    nx, ny, nz,
    tokens, latents, tok_gain, lat_gain, mlp_gain,
    w_ref_tok, w_val_tok, w_out_tok, w_ref_lat, w_val_lat, w_out_lat, w_up, w_down,
    tokens_out, latents_out,
    wtok, up, down, wlat, latx, wout, rvo, rv, lat_rv, km, vm, scores, cmax, acc, att_out, att,
    col_in, blk, rs, zb, lab, sq, sq_in, part, part_in, mid, mlp_in, hid, mp, mp_in,
    load, send, recv,
):
    ng = nx * ny
    nm = 2 * nz
    rows, width = tokens.shape
    g = lax.axis_index("group")
    m = lax.axis_index("member")
    z = lax.div(m, 2)
    c = lax.rem(m, 2)
    y = lax.div(g, nx)
    x = lax.rem(g, nx)
    other = 1 - c
    partner = (g, z * 2 + other)
    gpair = lax.div(g, 2)

    def remote(src, dst, slot, device):
        return pltpu.make_async_remote_copy(
            src_ref=src, dst_ref=dst, send_sem=send.at[min(slot, S_REF)] if isinstance(slot, int) else send.at[S_REF],
            recv_sem=recv.at[slot], device_id=device, device_id_type=MESH,
        )

    def local(src, dst, slot):
        return pltpu.make_async_copy(src, dst, recv.at[slot])

    def wait_recv(ref, slot):
        pltpu.make_async_copy(ref, ref, recv.at[slot]).wait()

    def wait_send(ref, slot):
        pltpu.make_async_copy(ref, ref, send.at[slot]).wait()

    def each(low, high, body):
        def step(i, carry):
            body(i)
            return carry

        lax.fori_loop(low, high, step, 0)

    def lanes(index, size=PAIR):
        return pl.ds(pl.multiple_of(index * size, size), size)

    def block_rows(index, size=64):
        return pl.ds(pl.multiple_of(index * size, size), size)

    loads = [
        pltpu.make_async_copy(w_ref_tok, wtok.at[0], load.at[0]),
        pltpu.make_async_copy(w_val_tok, wtok.at[1], load.at[1]),
        pltpu.make_async_copy(w_out_tok, wtok.at[2], load.at[2]),
        pltpu.make_async_copy(w_up, up.at[0], load.at[3]),
        pltpu.make_async_copy(w_down, down.at[0], load.at[4]),
    ]
    for item in loads:
        item.start()

    barrier = pltpu.get_barrier_semaphore()

    def greet(device):
        pl.semaphore_signal(barrier, inc=1, device_id=device, device_id_type=MESH)

    owner = lax.rem(z + gpair, nz)

    each(1, nm, lambda k: greet((g, lax.rem(m + k, nm))))
    each(1, ng, lambda k: greet((lax.rem(g + k, ng), m)))
    tok32 = tokens[...].astype(F32)
    tok_norm = (tok32 * scale_of(tok32) * tok_gain[...]).astype(BF16)

    def project_tokens(kind):
        for n in range(nz // 2):
            made = dot(tok_norm, wtok[kind, :, n * 256 : (n + 1) * 256]).astype(BF16)
            for i in range(2):
                rvo[kind, 2 * n + i] = made[:, i * PAIR : (i + 1) * PAIR]

    loads[0].wait()
    project_tokens(0)
    pl.semaphore_wait(barrier, nm + ng - 2)

    piece_rows = 64 // nx
    x_rows = block_rows(x, piece_rows)

    def send_w(k):
        zz = lax.rem(z + k, nz)
        remote(w_ref_lat.at[x_rows, lanes(zz)], wlat.at[m, x], S_W, (g, zz * 2)).start()
        remote(w_val_lat.at[x_rows, lanes(zz)], wlat.at[m, x], S_W, (g, zz * 2 + 1)).start()

    each(1, nz, send_w)

    @pl.when(c == 0)
    def _():
        local(w_ref_lat.at[x_rows, lanes(z)], wlat.at[m, x], S_W).start()
        remote(w_val_lat.at[x_rows, lanes(z)], wlat.at[m, x], S_W, partner).start()

    @pl.when(c == 1)
    def _():
        local(w_val_lat.at[x_rows, lanes(z)], wlat.at[m, x], S_W).start()
        remote(w_ref_lat.at[x_rows, lanes(z)], wlat.at[m, x], S_W, partner).start()

    high = nz // ny
    z_low = lax.rem(z, ny)
    z_high = lax.div(z, ny)
    for hh in range(high):
        zz = lax.rem(z_low + ny - y, ny) + ny * hh
        for cc in range(2):
            to_self = (zz == z) & (c == cc)

            @pl.when(to_self)
            def _():
                local(latents.at[x_rows, :], latx.at[z_high, c], S_LAT).start()

            @pl.when(jnp.logical_not(to_self))
            def _(zz=zz, cc=cc):
                remote(latents.at[x_rows, :], latx.at[z_high, c], S_LAT, (g, zz * 2 + cc)).start()

    up_rows = width // ng
    down_rows = down.shape[1] // ny
    down_cols = width // nx
    up_piece = block_rows(g, up_rows)
    down_piece = (block_rows(y, down_rows), lanes(x, down_cols))

    def send_mlp(k):
        device = (g, lax.rem(z + k, nz) * 2 + c)
        remote(w_up.at[up_piece, :], up.at[nz - k, up_piece, :], S_UP1, device).start()
        remote(
            w_down.at[down_piece[0], down_piece[1]],
            down.at[nz - k, down_piece[0], down_piece[1]], S_DOWN1, device,
        ).start()

    local(rvo.at[0, z], rv.at[0, 0], S_REF).start()

    def send_ref(k):
        zz = lax.rem(z + k, nz)
        remote(rvo.at[0, zz], rv.at[0, nz - k], S_REF + nz - k, (g, zz * 2 + c)).start()

    each(1, nz, send_ref)
    each(1, nz, send_mlp)

    def x_peer(k):
        return (y * nx + lax.rem(x + k, nx), m)

    def y_peer(k):
        return (lax.rem(y + k, ny) * nx + x, m)

    wait_recv(wlat.at[:, x], S_W)
    each(1, nx, lambda k: remote(wlat.at[:, x], wlat.at[:, x], S_W2, x_peer(k)).start())

    loads[1].wait()
    project_tokens(1)
    local(rvo.at[1, z], rv.at[1, 0], S_VAL).start()

    def send_val(k):
        zz = lax.rem(z + k, nz)
        remote(rvo.at[1, zz], rv.at[1, nz - k], S_VAL, (g, zz * 2 + c)).start()

    each(1, nz, send_val)

    def send_wout(k):
        device = (g, lax.rem(z + k, nz) * 2 + c)
        remote(w_out_lat.at[:, lanes(gpair)], wout.at[block_rows(k), :], S_WOUT, device).start()

    wait_recv(latx, S_LAT)
    lat32 = latx[...].reshape(64, width).astype(F32)
    lat_norm = (lat32 * scale_of(lat32) * lat_gain[...]).astype(BF16)
    wait_recv(wlat.at[:, pl.ds(0, nx - 1)], S_W2)
    made = dot(lat_norm, wlat[...].reshape(width, PAIR)).astype(BF16).reshape(high, 2, piece_rows, PAIR)
    low = lax.rem(z + y, ny)
    for hh in range(high):
        for cc in range(2):
            lat_rv[c, hh, low, cc, x] = made[hh, cc]

    def send_proj(k):
        block = lat_rv.at[c, :, low, :, x]
        remote(block, block, S_PROJ, (lax.rem(g + k, ng), m)).start()

    each(1, ng, send_proj)

    local(w_out_lat.at[:, lanes(gpair)], wout.at[pl.ds(0, 64), :], S_WOUT).start()
    each(1, nz, send_wout)

    rest = pl.ds(1, nz - 1)

    def up_x(index, part, parts):
        size = up_rows // parts
        return up.at[rest, block_rows((y * nx + index) * parts + part, size), :]

    def up_y(index, part, parts):
        size = nx * up_rows // parts
        return up.at[rest, block_rows(index * parts + part, size), :]

    def down_y(index, part, parts):
        size = down_rows // parts
        return down.at[rest, block_rows(index * parts + part, size), lanes(x, down_cols)]

    def down_x(index, part, parts):
        return down.at[rest, :, lanes(index * parts + part, down_cols // parts)]

    rings = {
        "ux": (nx, x, x_peer, up_x, S_RING),
        "dy": (ny, y, y_peer, down_y, S_RING + 4),
        "uy": (ny, y, y_peer, up_y, S_RING + 8),
        "dx": (nx, x, x_peer, down_x, S_RING + 12),
    }

    def ring_start(name):
        n, at, peer, block, slot = rings[name]
        for k in sorted({1, n - 1} - {0}):
            own = block(at, 0, 1)
            remote(own, own, slot + (k != 1), peer(k)).start()

    def ring_turn(name):
        n, at, peer, block, slot = rings[name]
        if n > 1:
            wait_recv(block(at, 0, 1), slot)
        if n == 4:
            left = block(lax.rem(at + 3, 4), 0, 2)
            remote(left, left, slot + 2, peer(1)).start()
            wait_recv(block(at, 0, 1), slot + 1)
            right = block(lax.rem(at + 1, 4), 1, 2)
            remote(right, right, slot + 3, peer(3)).start()

    def ring_end(name):
        n, at, peer, block, slot = rings[name]
        if n == 4:
            wait_recv(block(at, 0, 2), slot + 2)
            wait_recv(block(at, 0, 2), slot + 3)

    def ring_sent(name):
        n, at, peer, block, slot = rings[name]
        for k in sorted({1, n - 1} - {0}):
            wait_send(block(at, 0, 1), slot + (k != 1))
        if n == 4:
            wait_send(block(at, 0, 2), slot + 2)
            wait_send(block(at, 0, 2), slot + 3)

    wait_recv(up.at[rest, up_piece, :], S_UP1)
    wait_recv(down.at[rest, down_piece[0], down_piece[1]], S_DOWN1)
    ring_start("ux")
    ring_start("dy")

    others = lat_rv.at[0].reshape(ng * 64, PAIR).at[pl.ds(0, (ng - 1) * 64), :]
    wait_recv(others, S_PROJ)
    remote(lat_rv.at[c], lat_rv.at[c], S_PROJ2, partner).start()
    ring_turn("ux")
    ring_turn("dy")

    wait_recv(lat_rv.at[other], S_PROJ2)
    lat_count = ng * 64
    lane = lax.broadcasted_iota(jnp.int32, (lat_count, PAIR), 1)
    keys = lat_rv[0].reshape(lat_count, PAIR).astype(F32) * HEAD_DIM ** (-0.5)
    values = lat_rv[1].reshape(lat_count, PAIR).astype(F32)
    for h in range(2):
        mine = (lane < HEAD_DIM) if h == 0 else (lane >= HEAD_DIM)
        km[h] = jnp.where(mine, keys, 0.0).astype(BF16)
        vm[h] = jnp.where(mine, values, 0.0).astype(BF16)

    ring_end("ux")
    ring_end("dy")
    ring_start("uy")
    ring_start("dx")

    cmax[...] = jnp.full(cmax.shape, -jnp.inf, F32)
    pair_lanes = lanes(z)

    def place(i):
        half = lax.div(i + 1, 2)
        return jnp.where(lax.rem(i, 2) == 1, half, lax.rem(nz - half, nz))

    def score_block(i):
        k = place(i)
        wait_recv(rv.at[0, k], S_REF + k)
        query = rv[0, k]
        for h in range(2):
            score = lax.dot_general(query, km[h], (((1,), (1,)), ((), ())), preferred_element_type=F32)
            scores[h, k] = score
            cmax[h] = jnp.maximum(cmax[h], jnp.max(score.reshape(rows // 8, 8, lat_count), axis=0))

    each(0, nz, score_block)

    peaks = [jnp.max(cmax[h], axis=0, keepdims=True) for h in range(2)]
    acc[...] = jnp.zeros(acc.shape, F32)
    wait_recv(rv.at[1], S_VAL)

    def columns(t):
        pair = rv[1, pl.ds(2 * t, 2)].reshape(2 * rows, PAIR)
        turned = pair.astype(F32).T.astype(BF16)
        ones = jnp.ones((16, 2 * rows), BF16)
        for h in range(2):
            score = scores[h, pl.ds(2 * t, 2)].reshape(2 * rows, lat_count)
            exponent = jnp.exp(score - peaks[h]).astype(BF16)
            left = jnp.concatenate([turned[h * HEAD_DIM : (h + 1) * HEAD_DIM], ones], axis=0)
            acc[h] = acc[h] + dot(left, exponent)

    each(0, nz // 2, columns)
    for h in range(2):
        acc[h, 72:80, :] = jnp.broadcast_to(peaks[h], (8, lat_count))
    remote(acc.at[other], col_in, S_COL, partner).start()
    ring_turn("uy")
    ring_turn("dx")

    def attend(i):
        k = place(nz - 1 - i)
        result = jnp.zeros((rows, PAIR), F32)
        for h in range(2):
            score = scores[h, k]
            exponent = jnp.exp(score - jnp.max(score, axis=1, keepdims=True))
            inverse = 1.0 / jnp.sum(exponent, axis=1, keepdims=True)
            result = result + dot((exponent * inverse).astype(BF16), vm[h])
        att_out[k] = result.astype(BF16)

        @pl.when(k == 0)
        def _():
            local(att_out.at[0], att.at[:, pair_lanes], S_ATT).start()

        @pl.when(k > 0)
        def _():
            device = (g, lax.rem(z + k, nz) * 2 + c)
            remote(att_out.at[k], att.at[:, pair_lanes], S_ATT, device).start()

    each(0, nz // 4, attend)

    wait_recv(col_in, S_COL)
    own_peak = acc[c, 72:80, :]
    in_peak = col_in[72:80, :]
    peak = jnp.maximum(own_peak, in_peak)
    own_scale = jnp.exp(own_peak - peak)
    in_scale = jnp.exp(in_peak - peak)
    own_sums = acc[c, 0:72, :].reshape(9, 8, lat_count)
    in_sums = col_in[0:72, :].reshape(9, 8, lat_count)
    sums = (own_sums * own_scale[None] + in_sums * in_scale[None]).reshape(72, lat_count)
    for b in range(ng):
        span = slice((b // 2) * PAIR, (b // 2 + 1) * PAIR)
        blk[b, 0:32, :] = sums[(b % 2) * 32 : (b % 2) * 32 + 32, span]
        blk[b, 32:36, :] = sums[64:68, span]
        blk[b, 36:40, :] = peak[0:4, span]

    def block_of(gg):
        return 2 * lax.rem(z + lax.div(gg, 2), nz) + lax.rem(gg, 2)

    def send_blk(k):
        gg = lax.rem(g + k, ng)
        remote(blk.at[block_of(gg)], rs.at[g], S_RS, (gg, m)).start()

    local(blk.at[block_of(g)], rs.at[g], S_RS).start()
    each(1, ng, send_blk)

    each(nz // 4, nz, attend)

    wait_recv(rs, S_RS)
    all_peaks = rs[:, 36:37, :]
    factor = jnp.exp(all_peaks - jnp.max(all_peaks, axis=0, keepdims=True))
    total = jnp.sum(rs[:, 32:33, :] * factor, axis=0)
    summed = jnp.sum(rs[:, 0:32, :] * factor, axis=0)
    zb[...] = summed / total

    @pl.when(owner == z)
    def _():
        local(zb, lab.at[g], S_ZC).start()

    @pl.when(owner != z)
    def _():
        remote(zb, lab.at[g], S_ZC, (g, owner * 2 + c)).start()

    wait_recv(att, S_ATT)
    loads[2].wait()
    mid[...] = tokens[...].astype(F32) + dot(att[...], wtok[2])
    mid32 = mid[...]
    mlp_in[c] = (mid32 * scale_of(mid32) * mlp_gain[...]).astype(BF16)
    remote(mlp_in.at[c], mlp_in.at[c], S_MIN, partner).start()

    wait_recv(zb, S_ZC)

    def send_lab(k):
        remote(lab.at[g], lab.at[g], S_AG, (lax.rem(g + k, ng), m)).start()

    each(1, ng, send_lab)

    loads[3].wait()
    loads[4].wait()
    wait_recv(mlp_in.at[other], S_MIN)
    ring_end("uy")
    both = mlp_in[...].reshape(2 * rows, width)
    for n in range(nz // 2):
        piece = jnp.concatenate([up[2 * n], up[2 * n + 1]], axis=1)
        hid[:, n * 256 : (n + 1) * 256] = gelu(dot(both, piece)).astype(BF16)

    wait_recv(lab.at[pl.ds(0, ng - 1)], S_AG)
    attended = lab[...].reshape(ng * 32, PAIR)
    sq[...] = jnp.broadcast_to(jnp.sum(attended * attended, axis=0, keepdims=True), (8, PAIR))
    remote(sq, sq_in, S_SQ, partner).start()

    ring_end("dx")
    half_width = width // 2
    step = min(256, half_width)

    def mlp_out(first, last, slot):
        for n in range(first, last, step):
            span = slice(n, n + step)
            made = dot(hid[...], down[:, :, span].reshape(hid.shape[1], step))
            mp[:, :, span] = made.reshape(2, rows, step)
        span = pl.ds(first, last - first)
        remote(mp.at[other, :, span], mp_in.at[:, span], slot, partner).start()

    mlp_out(0, half_width, S_MP0)

    wait_recv(sq_in, S_SQ)
    norm = lax.rsqrt((sq[0:1, :] + sq_in[0:1, :]) * (1.0 / width) + NORM_EPS)
    mixed = (attended * norm).T.astype(BF16)
    wait_recv(wout, S_WOUT)
    part[...] = dot(mixed, wout[...]).reshape(2, 64, PAIR)
    remote(part.at[other], part_in, S_PART, partner).start()

    mlp_out(half_width, width, S_MP1)

    wait_recv(part_in, S_PART)
    own_lanes = lanes(gpair)
    latents_out[:, own_lanes] = (
        latents[:, own_lanes].astype(F32) + (part[c] + part_in[...])
    ).astype(BF16)

    def send_lo(k):
        device = (2 * lax.rem(gpair + k, nz) + lax.rem(g, 2), m)
        remote(latents_out.at[:, own_lanes], latents_out.at[:, own_lanes], S_LO, device).start()

    each(1, nz, send_lo)

    for first, slot in ((0, S_MP0), (half_width, S_MP1)):
        span = slice(first, first + half_width)
        wait_recv(mp_in.at[:, pl.ds(first, half_width)], slot)
        tokens_out[:, span] = (mid[:, span] + (mp[c, :, span] + mp_in[:, span])).astype(BF16)

    wait_recv(latents_out.at[:, pl.ds(0, (nz - 1) * PAIR)], S_LO)

    @pl.when(y != 0)
    def _():
        wait_send(latx.at[0, 0], S_LAT)

    for _ in range(2 * high - 1):
        wait_send(latx.at[0, 0], S_LAT)

    @pl.when(owner != z)
    def _():
        wait_send(zb, S_ZC)

    wait_send(lab.at[pl.ds(0, ng - 1)], S_AG)
    wait_send(wlat.at[pl.ds(0, nm - 1), 0], S_W)
    wait_send(wlat.at[:, pl.ds(0, nx - 1)], S_W2)
    wait_send(up.at[rest, up_piece, :], S_UP1)
    wait_send(down.at[rest, down_piece[0], down_piece[1]], S_DOWN1)
    wait_send(rv.at[0, rest], S_REF)
    wait_send(rv.at[1, rest], S_VAL)
    wait_send(wout.at[pl.ds(0, (nz - 1) * 64), :], S_WOUT)
    wait_send(others, S_PROJ)
    wait_send(lat_rv.at[0], S_PROJ2)
    for name in rings:
        ring_sent(name)
    wait_send(att_out.at[pl.ds(1, nz - 1)], S_ATT)
    wait_send(col_in, S_COL)
    wait_send(mlp_in.at[0], S_MIN)
    wait_send(rs.at[pl.ds(0, ng - 1)], S_RS)
    wait_send(sq_in, S_SQ)
    wait_send(part_in, S_PART)
    wait_send(mp_in.at[:, pl.ds(0, half_width)], S_MP0)
    wait_send(mp_in.at[:, pl.ds(half_width, half_width)], S_MP1)
    wait_send(latents_out.at[:, pl.ds(0, (nz - 1) * PAIR)], S_LO)


def per_device(nx, ny, nz, *args):
    (tokens, latents, tok_gain, lat_gain, mlp_gain, *weights) = args
    ng = nx * ny
    rows, width = tokens.shape
    lat_count = latents.shape[0] * 2 * nz
    unit = weights[6].shape[1]
    vmem = pl.BlockSpec(memory_space=pltpu.VMEM)
    anywhere = pl.BlockSpec(memory_space=pl.ANY)
    scratch = [
        ((3, width, width), BF16),
        ((nz, width, unit), BF16),
        ((nz, unit, width), BF16),
        ((2 * nz, nx, 64 // nx, PAIR), BF16),
        ((nz // ny, 2, 64 // nx, width), BF16),
        ((nz * 64, PAIR), BF16),
        ((2, nz, rows, PAIR), BF16),
        ((2, nz, rows, PAIR), BF16),
        ((2, nz // ny, ny, 2, nx, 64 // nx, PAIR), BF16),
        ((2, lat_count, PAIR), BF16),
        ((2, lat_count, PAIR), BF16),
        ((2, nz, rows, lat_count), F32),
        ((2, 8, lat_count), F32),
        ((2, 80, lat_count), F32),
        ((nz, rows, PAIR), BF16),
        ((rows, width), BF16),
        ((80, lat_count), F32),
        ((ng, 40, PAIR), F32),
        ((ng, 40, PAIR), F32),
        ((32, PAIR), F32),
        ((ng, 32, PAIR), F32),
        ((8, PAIR), F32),
        ((8, PAIR), F32),
        ((2, 64, PAIR), F32),
        ((64, PAIR), F32),
        ((rows, width), F32),
        ((2, rows, width), BF16),
        ((2 * rows, nz * unit), BF16),
        ((2, rows, width), F32),
        ((rows, width), F32),
    ]
    return pl.pallas_call(
        functools.partial(kernel, nx, ny, nz),
        out_shape=(
            jax.ShapeDtypeStruct(tokens.shape, BF16),
            jax.ShapeDtypeStruct(latents.shape, BF16),
        ),
        in_specs=[vmem] * 5 + [anywhere] * 8,
        out_specs=(vmem, vmem),
        scratch_shapes=[pltpu.VMEM(shape, kind) for shape, kind in scratch]
        + [
            pltpu.SemaphoreType.DMA((5,)),
            pltpu.SemaphoreType.DMA((S_REF + 1,)),
            pltpu.SemaphoreType.DMA((S_REF + nz,)),
        ],
        compiler_params=pltpu.CompilerParams(
            collective_id=0, has_side_effects=True, vmem_limit_bytes=56 * 1024 * 1024
        ),
        name="layer",
    )(
        tokens,
        latents,
        tok_gain.reshape(1, width),
        lat_gain.reshape(1, width),
        mlp_gain.reshape(1, width),
        *weights,
    )


def solution(mesh):
    ng = mesh.shape["group"]
    nz = mesh.shape["member"] // 2
    nx = int(round(ng**0.5))
    in_specs = (
        P(("group", "member"), None),
        P("member", None),
        P(),
        P(),
        P(),
        P(),
        P(),
        P(),
        P("member", None),
        P("member", None),
        P("member", None),
        P(None, "member"),
        P("member", None),
    )
    out_specs = (P(("group", "member"), None), P("member", None))
    return jax.shard_map(
        functools.partial(per_device, nx, ng // nx, nz),
        mesh=mesh, in_specs=in_specs, out_specs=out_specs, check_vma=False,
    )
```

time: 97 us -> 83.9 us (0.86)
  Pallas kernels: 92.1 us -> 79.9 us
    pallas_call x1, Pallas kernels: 92.1 us -> 79.9 us  [per_device(): pl.pallas_call(functools.partial(kernel, nx, ny, nz), out_shape=(jax.Shap...]
where the time goes in v2:
time: 83.9 us; the launch traced here: 83.8 us
  Pallas kernels  79.9 us (95%)
  local copies, waits for them, and re-layouts  3.24 us (4%)
    pallas_call x1, Pallas kernels, per_device(): pl.pallas_call(functools.partial(kernel, nx, ny, nz), out_shape=(jax.Shap...  79.9 us
    unnamed x2, local copies, waits for them, and re-layouts  3.24 us

profile of v2, /device:TPU:1, one launch (start us, length us, event | category | flops | bytes accessed | tf_op | source)
XLA Modules:
  0.0 83.8 jit_solution(3555115504493519790)
XLA Ops:
  0.6 79.9 %layer.1 = (bf16[128,1024]{1,0:T(8,128)(2,1)}, bf16[64,1024]{1,0:T(8,128)(2,1)}) custom-call(bf16[128,1024]{1,0:T(8,128)(2,1)} %tokens.1, bf16[64,1024]{1,0:T(8,128)(2,1)} %latents.1, f32[1,1024]{1,0:T(1,128)} %bitcast.3, f32[1,1024]{1,0:T(1,128)} %bitcast.4, f32[1,1024]{1,0:T(1,128)} %bitcast.5, bf16[1024,1024]{1,0:T(8,128)(2,1)} %w_ref_tok.1, ...), custom_call_target="tpu_custom_call" | custom-call | tf_op jit(solution)/shard_map/layer/pallas_call | solution.py:547
  80.6 1.7 %copy.17 = bf16[128,1024]{1,0:T(8,128)(2,1)} copy(bf16[128,1024]{1,0:T(8,128)(2,1)} %get-tuple-element.4) | data formatting | bytes 524288
  82.2 1.6 %copy.18 = bf16[64,1024]{1,0:T(8,128)(2,1)} copy(bf16[64,1024]{1,0:T(8,128)(2,1)} %get-tuple-element.5) | data formatting | bytes 262144

commit v3 on v2

--- a/solution.py
+++ b/solution.py
@@ -166,6 +166,7 @@
             down.at[nz - k, down_piece[0], down_piece[1]], S_DOWN1, device,
         ).start()
 
+    each(1, nz, send_mlp)
     local(rvo.at[0, z], rv.at[0, 0], S_REF).start()
 
     def send_ref(k):
@@ -173,7 +174,6 @@
         remote(rvo.at[0, zz], rv.at[0, nz - k], S_REF + nz - k, (g, zz * 2 + c)).start()
 
     each(1, nz, send_ref)
-    each(1, nz, send_mlp)
 
     def x_peer(k):
         return (y * nx + lax.rem(x + k, nx), m)
@@ -334,8 +334,6 @@
     for h in range(2):
         acc[h, 72:80, :] = jnp.broadcast_to(peaks[h], (8, lat_count))
     remote(acc.at[other], col_in, S_COL, partner).start()
-    ring_turn("uy")
-    ring_turn("dx")
 
     def attend(i):
         k = place(nz - 1 - i)
@@ -400,6 +398,8 @@
     def _():
         remote(zb, lab.at[g], S_ZC, (g, owner * 2 + c)).start()
 
+    ring_turn("uy")
+    ring_turn("dx")
     wait_recv(att, S_ATT)
     loads[2].wait()
     mid[...] = tokens[...].astype(F32) + dot(att[...], wtok[2])

time: 83.9 us -> 72.3 us (0.86)
  Pallas kernels: 79.9 us -> 68.2 us
    pallas_call x1, Pallas kernels: 79.9 us -> 68.2 us  [per_device(): pl.pallas_call(functools.partial(kernel, nx, ny, nz), out_shape=(jax.Shap...]
where the time goes in v3:
time: 72.3 us; the launch traced here: 72.1 us
  Pallas kernels  68.2 us (94%)
  local copies, waits for them, and re-layouts  3.24 us (4%)
    pallas_call x1, Pallas kernels, per_device(): pl.pallas_call(functools.partial(kernel, nx, ny, nz), out_shape=(jax.Shap...  68.2 us
    unnamed x2, local copies, waits for them, and re-layouts  3.24 us

profile of v3, /device:TPU:1, one launch (start us, length us, event | category | flops | bytes accessed | tf_op | source)
XLA Modules:
  0.0 72.1 jit_solution(896426595007986805)
XLA Ops:
  0.6 68.2 %layer.1 = (bf16[128,1024]{1,0:T(8,128)(2,1)}, bf16[64,1024]{1,0:T(8,128)(2,1)}) custom-call(bf16[128,1024]{1,0:T(8,128)(2,1)} %tokens.1, bf16[64,1024]{1,0:T(8,128)(2,1)} %latents.1, f32[1,1024]{1,0:T(1,128)} %bitcast.3, f32[1,1024]{1,0:T(1,128)} %bitcast.4, f32[1,1024]{1,0:T(1,128)} %bitcast.5, bf16[1024,1024]{1,0:T(8,128)(2,1)} %w_ref_tok.1, ...), custom_call_target="tpu_custom_call" | custom-call | tf_op jit(solution)/shard_map/layer/pallas_call | solution.py:547
  68.9 1.7 %copy.17 = bf16[128,1024]{1,0:T(8,128)(2,1)} copy(bf16[128,1024]{1,0:T(8,128)(2,1)} %get-tuple-element.4) | data formatting | bytes 524288
  70.5 1.6 %copy.18 = bf16[64,1024]{1,0:T(8,128)(2,1)} copy(bf16[64,1024]{1,0:T(8,128)(2,1)} %get-tuple-element.5) | data formatting | bytes 262144

commit v4 on v3

--- a/solution.py
+++ b/solution.py
@@ -286,12 +286,14 @@
     wait_recv(lat_rv.at[other], S_PROJ2)
     lat_count = ng * 64
     lane = lax.broadcasted_iota(jnp.int32, (lat_count, PAIR), 1)
+
+    def keep_head(array, h):
+        mine = (lane < HEAD_DIM) if h == 0 else (lane >= HEAD_DIM)
+        return jnp.where(mine, array, 0.0).astype(BF16)
+
     keys = lat_rv[0].reshape(lat_count, PAIR).astype(F32) * HEAD_DIM ** (-0.5)
-    values = lat_rv[1].reshape(lat_count, PAIR).astype(F32)
     for h in range(2):
-        mine = (lane < HEAD_DIM) if h == 0 else (lane >= HEAD_DIM)
-        km[h] = jnp.where(mine, keys, 0.0).astype(BF16)
-        vm[h] = jnp.where(mine, values, 0.0).astype(BF16)
+        km[h] = keep_head(keys, h)
 
     ring_end("ux")
     ring_end("dy")
@@ -334,6 +336,10 @@
     for h in range(2):
         acc[h, 72:80, :] = jnp.broadcast_to(peaks[h], (8, lat_count))
     remote(acc.at[other], col_in, S_COL, partner).start()
+
+    values = lat_rv[1].reshape(lat_count, PAIR).astype(F32)
+    for h in range(2):
+        vm[h] = keep_head(values, h)
 
     def attend(i):
         k = place(nz - 1 - i)
@@ -400,19 +406,19 @@
 
     ring_turn("uy")
     ring_turn("dx")
+    wait_recv(zb, S_ZC)
+
+    def send_lab(k):
+        remote(lab.at[g], lab.at[g], S_AG, (lax.rem(g + k, ng), m)).start()
+
+    each(1, ng, send_lab)
+
     wait_recv(att, S_ATT)
     loads[2].wait()
     mid[...] = tokens[...].astype(F32) + dot(att[...], wtok[2])
     mid32 = mid[...]
     mlp_in[c] = (mid32 * scale_of(mid32) * mlp_gain[...]).astype(BF16)
     remote(mlp_in.at[c], mlp_in.at[c], S_MIN, partner).start()
-
-    wait_recv(zb, S_ZC)
-
-    def send_lab(k):
-        remote(lab.at[g], lab.at[g], S_AG, (lax.rem(g + k, ng), m)).start()
-
-    each(1, ng, send_lab)
 
     loads[3].wait()
     loads[4].wait()

time: 72.3 us -> 72.3 us (level)
  no operation moved by 1% of the time
where the time goes in v4:
time: 72.3 us; the launch traced here: 72.1 us
  Pallas kernels  68.2 us (94%)
  local copies, waits for them, and re-layouts  3.24 us (4%)
    pallas_call x1, Pallas kernels, per_device(): pl.pallas_call(functools.partial(kernel, nx, ny, nz), out_shape=(jax.Shap...  68.2 us
    unnamed x2, local copies, waits for them, and re-layouts  3.24 us

profile of v4, /device:TPU:1, one launch (start us, length us, event | category | flops | bytes accessed | tf_op | source)
XLA Modules:
  0.0 72.1 jit_solution(14835252550521193388)
XLA Ops:
  0.6 68.2 %layer.1 = (bf16[128,1024]{1,0:T(8,128)(2,1)}, bf16[64,1024]{1,0:T(8,128)(2,1)}) custom-call(bf16[128,1024]{1,0:T(8,128)(2,1)} %tokens.1, bf16[64,1024]{1,0:T(8,128)(2,1)} %latents.1, f32[1,1024]{1,0:T(1,128)} %bitcast.3, f32[1,1024]{1,0:T(1,128)} %bitcast.4, f32[1,1024]{1,0:T(1,128)} %bitcast.5, bf16[1024,1024]{1,0:T(8,128)(2,1)} %w_ref_tok.1, ...), custom_call_target="tpu_custom_call" | custom-call | tf_op jit(solution)/shard_map/layer/pallas_call | solution.py:553
  68.9 1.7 %copy.17 = bf16[128,1024]{1,0:T(8,128)(2,1)} copy(bf16[128,1024]{1,0:T(8,128)(2,1)} %get-tuple-element.4) | data formatting | bytes 524288
  70.6 1.6 %copy.18 = bf16[64,1024]{1,0:T(8,128)(2,1)} copy(bf16[64,1024]{1,0:T(8,128)(2,1)} %get-tuple-element.5) | data formatting | bytes 262144

commit v5 on v4

--- a/solution.py
+++ b/solution.py
@@ -41,7 +41,7 @@
     tokens_out, latents_out,
     wtok, up, down, wlat, latx, wout, rvo, rv, lat_rv, km, vm, scores, cmax, acc, att_out, att,
     col_in, blk, rs, zb, lab, sq, sq_in, part, part_in, mid, mlp_in, hid, mp, mp_in,
-    load, send, recv,
+    load, send, recv, heard,
 ):
     ng = nx * ny
     nm = 2 * nz
@@ -94,6 +94,12 @@
     for item in loads:
         item.start()
 
+    def x_peer(k):
+        return (y * nx + lax.rem(x + k, nx), m)
+
+    def y_peer(k):
+        return (lax.rem(y + k, ny) * nx + x, m)
+
     barrier = pltpu.get_barrier_semaphore()
 
     def greet(device):
@@ -101,8 +107,10 @@
 
     owner = lax.rem(z + gpair, nz)
 
-    each(1, nm, lambda k: greet((g, lax.rem(m + k, nm))))
-    each(1, ng, lambda k: greet((lax.rem(g + k, ng), m)))
+    greet(partner)
+    each(1, nz, lambda k: greet((g, lax.rem(z + k, nz) * 2 + c)))
+    each(1, nx, lambda k: greet(x_peer(k)))
+    each(1, ny, lambda k: greet(y_peer(k)))
     tok32 = tokens[...].astype(F32)
     tok_norm = (tok32 * scale_of(tok32) * tok_gain[...]).astype(BF16)
 
@@ -114,27 +122,36 @@
 
     loads[0].wait()
     project_tokens(0)
-    pl.semaphore_wait(barrier, nm + ng - 2)
+    pl.semaphore_wait(barrier, nz + nx - 1 + ny - 1)
+
+    def tell(sem, device):
+        pl.semaphore_signal(sem, inc=1, device_id=device, device_id_type=MESH)
+
+    tell(heard.at[0], partner)
+    each(1, ny, lambda k: tell(heard.at[1], y_peer(k)))
 
     piece_rows = 64 // nx
     x_rows = block_rows(x, piece_rows)
 
-    def send_w(k):
-        zz = lax.rem(z + k, nz)
-        remote(w_ref_lat.at[x_rows, lanes(zz)], wlat.at[m, x], S_W, (g, zz * 2)).start()
-        remote(w_val_lat.at[x_rows, lanes(zz)], wlat.at[m, x], S_W, (g, zz * 2 + 1)).start()
-
-    each(1, nz, send_w)
-
-    @pl.when(c == 0)
-    def _():
-        local(w_ref_lat.at[x_rows, lanes(z)], wlat.at[m, x], S_W).start()
-        remote(w_val_lat.at[x_rows, lanes(z)], wlat.at[m, x], S_W, partner).start()
-
-    @pl.when(c == 1)
-    def _():
-        local(w_val_lat.at[x_rows, lanes(z)], wlat.at[m, x], S_W).start()
-        remote(w_ref_lat.at[x_rows, lanes(z)], wlat.at[m, x], S_W, partner).start()
+    def send_w(core):
+        source = w_val_lat if core else w_ref_lat
+
+        def send_one(k):
+            zz = lax.rem(z + k, nz)
+            remote(source.at[x_rows, lanes(zz)], wlat.at[m, x], S_W, (g, zz * 2 + core)).start()
+
+        each(1, nz, send_one)
+
+    for core in range(2):
+
+        @pl.when(c == core)
+        def _(core=core):
+            source, across = (w_val_lat, w_ref_lat) if core else (w_ref_lat, w_val_lat)
+            local(source.at[x_rows, lanes(z)], wlat.at[m, x], S_W).start()
+            send_w(core)
+            remote(across.at[x_rows, lanes(z)], wlat.at[m, x], S_W, partner).start()
+            pl.semaphore_wait(heard.at[0], 1)
+            send_w(1 - core)
 
     high = nz // ny
     z_low = lax.rem(z, ny)
@@ -174,12 +191,6 @@
         remote(rvo.at[0, zz], rv.at[0, nz - k], S_REF + nz - k, (g, zz * 2 + c)).start()
 
     each(1, nz, send_ref)
-
-    def x_peer(k):
-        return (y * nx + lax.rem(x + k, nx), m)
-
-    def y_peer(k):
-        return (lax.rem(y + k, ny) * nx + x, m)
 
     wait_recv(wlat.at[:, x], S_W)
     each(1, nx, lambda k: remote(wlat.at[:, x], wlat.at[:, x], S_W2, x_peer(k)).start())
@@ -212,6 +223,7 @@
         block = lat_rv.at[c, :, low, :, x]
         remote(block, block, S_PROJ, (lax.rem(g + k, ng), m)).start()
 
+    pl.semaphore_wait(heard.at[1], ny - 1)
     each(1, ng, send_proj)
 
     local(w_out_lat.at[:, lanes(gpair)], wout.at[pl.ds(0, 64), :], S_WOUT).start()
@@ -563,6 +575,7 @@
             pltpu.SemaphoreType.DMA((5,)),
             pltpu.SemaphoreType.DMA((S_REF + 1,)),
             pltpu.SemaphoreType.DMA((S_REF + nz,)),
+            pltpu.SemaphoreType.REGULAR((2,)),
         ],
         compiler_params=pltpu.CompilerParams(
             collective_id=0, has_side_effects=True, vmem_limit_bytes=56 * 1024 * 1024

time: 72.3 us -> 71.9 us (level)
  no operation moved by 1% of the time
where the time goes in v5:
time: 71.9 us; the launch traced here: 71.8 us
  Pallas kernels  67.9 us (94%)
  local copies, waits for them, and re-layouts  3.24 us (5%)
    pallas_call x1, Pallas kernels, per_device(): pl.pallas_call(functools.partial(kernel, nx, ny, nz), out_shape=(jax.Shap...  67.9 us
    unnamed x2, local copies, waits for them, and re-layouts  3.24 us

profile of v5, /device:TPU:1, one launch (start us, length us, event | category | flops | bytes accessed | tf_op | source)
XLA Modules:
  0.0 71.8 jit_solution(10365250890984413542)
XLA Ops:
  0.6 67.9 %layer.1 = (bf16[128,1024]{1,0:T(8,128)(2,1)}, bf16[64,1024]{1,0:T(8,128)(2,1)}) custom-call(bf16[128,1024]{1,0:T(8,128)(2,1)} %tokens.1, bf16[64,1024]{1,0:T(8,128)(2,1)} %latents.1, f32[1,1024]{1,0:T(1,128)} %bitcast.3, f32[1,1024]{1,0:T(1,128)} %bitcast.4, f32[1,1024]{1,0:T(1,128)} %bitcast.5, bf16[1024,1024]{1,0:T(8,128)(2,1)} %w_ref_tok.1, ...), custom_call_target="tpu_custom_call" | custom-call | tf_op jit(solution)/shard_map/layer/pallas_call | solution.py:565
  68.6 1.7 %copy.17 = bf16[128,1024]{1,0:T(8,128)(2,1)} copy(bf16[128,1024]{1,0:T(8,128)(2,1)} %get-tuple-element.4) | data formatting | bytes 524288
  70.2 1.6 %copy.18 = bf16[64,1024]{1,0:T(8,128)(2,1)} copy(bf16[64,1024]{1,0:T(8,128)(2,1)} %get-tuple-element.5) | data formatting | bytes 262144
